TPU v7x, 32 devices: a whole 2x2x4 slice. The times are simulated.
32 devices in a mesh: frag: 1, aux: 32 (over z, y, x, core), occ: 1.
Axes of the slice: x: 2, y: 2, z: 4, core: 2. Of those that a mesh axis runs over, the one named last changes fastest.
Arguments:
- integrals: bfloat16 [1280, 4, 128, 128], P(('frag', 'aux')), may hold values from -1 to 1
- block_list: int32 [1280, 3], P(('frag', 'aux')), may hold values from 0 to 1023, as said below
- block_count: int32 [32], P(('frag', 'aux')), may hold values from 30 to 40, as said below
- coeffs: bfloat16 [768, 128], P('frag', 'occ'), may hold values from -6 to 6
Outputs:
- exchange_matrix: float32 [768, 768], P(('frag', 'aux', 'occ'))
Inputs may be any that keep to these rules, and one draw needn't show every extreme that they name: block_list[r] = (a, u, v) with a < 1024 and u, v < 6. Auxiliary block a belongs to slab a // 32. Among the live rows of one slab at most 2 name auxiliary blocks of one slab, and in every draw some slab receives exactly 2 from every slab. Rows past a slab's count hold valid indices but are not used. `block_count`: live rows come first on each slab; some slab is full in every draw.
All inputs are finite; a program needn't handle non-finite values.
Results may differ from a plain program's by a relative error of at most 0.0003.
Values may be sent and summed in bfloat16 or wider, within the bound.
A program may use at most 128 MiB of HBM per device.

v0:
```python
import jax
import jax.numpy as jnp
from jax import lax
from jax.sharding import PartitionSpec as P

AUX_DEV = 128
OCC = 128


def body(integrals, block_list, block_count, coeffs):
    stored, aux_width, block_size, _ = integrals.shape
    basis, occ_local = coeffs.shape
    basis_blocks = basis // block_size
    aux_nodes = lax.axis_size("aux")
    owned_blocks = AUX_DEV // aux_width
    slot_count = max(2, 64 // aux_nodes)
    segments = owned_blocks * basis_blocks
    coef_blocks = coeffs.reshape(basis_blocks, block_size, occ_local)
    positions = jnp.arange(stored, dtype=jnp.int32)
    is_live = positions < block_count[0]
    owner_slab = jnp.where(is_live, block_list[:, 0] // owned_blocks, aux_nodes)
    member = (owner_slab[:, None] == jnp.arange(aux_nodes, dtype=jnp.int32)[None, :]).astype(
        jnp.int32
    )
    earlier = jnp.cumsum(member, axis=0) - member
    placed = jnp.sum(earlier * member, axis=1)
    target = jnp.where(is_live, owner_slab * slot_count + placed, aux_nodes * slot_count)
    source = (
        jnp.full((aux_nodes * slot_count + 1,), stored, jnp.int32)
        .at[target]
        .set(positions)[: aux_nodes * slot_count]
    )
    blank_tag = jnp.full((1, 3), -1, jnp.int32)
    send_tags = jnp.concatenate([block_list, blank_tag], axis=0)[source].reshape(
        aux_nodes, slot_count, 3
    )
    recv_tags = lax.all_to_all(send_tags, "aux", split_axis=0, concat_axis=0, tiled=True).reshape(
        aux_nodes * slot_count, 3
    )
    filled = recv_tags[:, 1] >= 0
    seg_of = jnp.where(
        filled, recv_tags[:, 1] * owned_blocks + recv_tags[:, 0] % owned_blocks, segments
    )
    seg_table = (jnp.arange(segments, dtype=jnp.int32)[:, None] == seg_of[None, :]).astype(
        jnp.bfloat16
    )
    padded = jnp.concatenate(
        [integrals, jnp.zeros((1,) + integrals.shape[1:], jnp.bfloat16)], axis=0
    )
    outgoing = padded[source].reshape(aux_nodes, slot_count, aux_width, block_size, block_size)
    lam_index = jnp.where(filled, recv_tags[:, 2], 0)
    recv_coef = coef_blocks[lam_index]
    item_block = lax.all_to_all(outgoing, "aux", split_axis=0, concat_axis=0, tiled=True)
    item_count = item_block.shape[2]
    flat_ints = item_block.reshape(aux_nodes * slot_count, item_count, block_size, block_size)
    half_rows = lax.dot_general(
        flat_ints, recv_coef, (((3,), (1,)), ((0,), (0,))), preferred_element_type=jnp.float32
    ).astype(jnp.bfloat16)
    summed = jnp.dot(
        seg_table, half_rows.reshape(aux_nodes * slot_count, -1), preferred_element_type=jnp.float32
    )
    fitted = summed.reshape(segments, item_count, block_size, occ_local)
    fitted = fitted.astype(jnp.bfloat16).reshape(
        basis_blocks, owned_blocks, aux_width, block_size, occ_local
    )
    fitted = fitted.transpose(0, 3, 1, 2, 4).reshape(basis, owned_blocks * aux_width * occ_local)
    scale_factor = 1.0 / (AUX_DEV * aux_nodes * OCC)
    return lax.psum_scatter(
        lax.dot_general(
            fitted, fitted, (((1,), (1,)), ((), ())), preferred_element_type=jnp.float32
        )
        * scale_factor,
        ("aux", "occ"),
        scatter_dimension=0,
        tiled=True,
    )


def solution(mesh):
    placed = (
        P(("frag", "aux"), None, None, None),
        P(("frag", "aux"), None),
        P(("frag", "aux")),
        P("frag", "occ"),
    )
    return jax.shard_map(
        body, mesh=mesh, in_specs=placed, out_specs=P(("frag", "aux", "occ"), None), check_vma=False
    )
```

profile of v0, /device:TPU:0, one launch (start us, length us, event | category | flops | bytes accessed | tf_op | source)
XLA Modules:
  0.0 478.2 jit_solution(11105299784345977320)
XLA Ops:
  6.5 0.0 copy-start
  7.2 0.8 copy.11
  8.0 0.7 fusion.16
  8.7 0.1 fusion.5
  8.8 0.1 reduce_window_sum.11
  8.8 0.2 select_reduce_fusion
  9.0 0.7 fusion.8
  9.7 0.7 scatter_custom_fusion
  10.5 1.2 gather_fusion
  11.7 7.3 %all-to-all-start = ((s32[32,2,3]{2,1,0:T(2,128)}), s32[32,2,3]{2,1,0:T(2,128)S(1)}, u32[]{:S(2)}, u32[]{:S(2)}) async-start(s32[32,2,3]{2,1,0:T(2,128)} %bitcast.4), calls=%async_computation | async-start | bytes 65536 | tf_op jit(solution)/shard_map/all_to_all | solution.py:37
  19.0 7.0 %concatenate.7 = bf16[41,4,128,128]{3,2,1,0:T(8,128)(2,1)} pad(bf16[40,4,128,128]{3,2,1,0:T(8,128)(2,1)} %param.4, bf16[]{:T(256)} %constant.52.clone.1), padding=0_1x0_0x0_0x0_0 | pad | bytes 10616834 | tf_op jit(solution)/shard_map/concatenate | solution.py:47
  25.9 8.0 %gather_fusion.1 = bf16[64,4,128,128]{3,2,1,0:T(8,128)(2,1)} fusion(bf16[41,4,128,128]{3,2,1,0:T(8,128)(2,1)} %concatenate.7, s32[1024]{0:T(1024)S(1)} %pad_clamp_fusion.1), kind=kCustom, calls=%fused_computation.1 | custom fusion | bytes 16777472 | tf_op jit(solution)/shard_map/gather | solution.py:50
  33.9 0.0 all-to-all-done
  33.9 5.9 %all-to-all-start.1 = ((bf16[32,2,4,128,128]{4,3,2,1,0:T(8,128)(2,1)}), bf16[32,2,4,128,128]{4,3,2,1,0:T(8,128)(2,1)}, u32[]{:S(2)}, u32[]{:S(2)}) async-start(bf16[32,2,4,128,128]{4,3,2,1,0:T(8,128)(2,1)} %bitcast.59), calls=%async_computation.1 | async-start | bytes 16777216 | tf_op jit(solution)/shard_map/all_to_all | solution.py:53
  39.8 0.2 reduce-scatter.2.cloned.1.call-start
  40.1 0.1 fusion.12
  40.1 0.1 copy.19
  40.2 0.1 copy.18
  40.3 0.1 copy.20
  40.4 0.0 copy-done
  40.4 1.0 gather_fusion.2
  41.4 184.5 %all-to-all-done.1 = bf16[32,2,4,128,128]{4,3,2,1,0:T(8,128)(2,1)} async-done(((bf16[32,2,4,128,128]{4,3,2,1,0:T(8,128)(2,1)}), bf16[32,2,4,128,128]{4,3,2,1,0:T(8,128)(2,1)}, u32[]{:S(2)}, u32[]{:S(2)}) %all-to-all-start.1) | async-done | bytes 8388640 | tf_op jit(solution)/shard_map/all_to_all | solution.py:53
  225.9 8.9 %convolution_convert_fusion.1 = bf16[64,4,128,128]{3,2,1,0:T(8,128)(2,1)} fusion(bf16[64,4,128,128]{3,2,1,0:T(8,128)(2,1)} %bitcast.12, bf16[64,128,128]{2,1,0:T(8,128)(2,1)S(1)} %gather_fusion.2), kind=kOutput, calls=%fused_computation.8 | convolution fusion | flops 1077936128 | bytes 18874368 | tf_op jit(solution)/shard_map/dot_general | solution.py:56
  234.8 12.0 %copy.28 = bf16[8,8,512,128]{3,1,2,0:T(8,128)(2,1)} copy(bf16[8,8,512,128]{3,2,1,0:T(8,128)(2,1)} %bitcast.60) | data formatting | bytes 16777216
  246.8 8.9 %copy.22 = bf16[8,8,512,128]{3,2,1,0:T(8,128)(2,1)} copy(bf16[8,8,512,128]{3,1,2,0:T(8,128)(2,1)} %copy.28) | data formatting | bytes 16777216
  255.7 18.1 %convolution_convert_fusion = bf16[192,4,128,128]{3,0,2,1:T(8,128)(2,1)} fusion(bf16[4,128,128,64]{2,1,0,3:T(8,128)(2,1)} %bitcast.58, s32[64]{0:T(128)S(1)} %bitcast_select_fusion), kind=kOutput, calls=%fused_computation.5 | convolution fusion | flops 1623207936 | bytes 33554688 | tf_op jit(solution)/shard_map/dot_general | solution.py:59
  273.8 32.3 %copy.27 = bf16[6,32,4,128,128]{4,2,1,3,0:T(4,128)(2,1)} copy(bf16[6,32,4,128,128]{4,1,0,3,2:T(8,128)(2,1)} %bitcast.56) | data formatting | bytes 50331648 | tf_op jit(solution)/shard_map/reshape | solution.py:63
  306.1 41.0 %reshape.78 = bf16[768,16384]{1,0:T(8,128)(2,1)} reshape(bf16[6,128,32,4,128]{4,3,2,1,0:T(4,128)(2,1)} %bitcast.57) | data formatting | bytes 50331648 | tf_op jit(solution)/shard_map/reshape | solution.py:66
  347.1 0.0 copy-start.1
  347.1 28.1 %convolution_multiply_fusion = f32[768,768]{1,0:T(8,128)} fusion(bf16[768,16384]{1,0:T(8,128)(2,1)} %reshape.78), kind=kOutput, calls=%fused_computation.10 | convolution fusion | flops 19327942656 | bytes 27525120 | tf_op jit(solution)/shard_map/dot_general | solution.py:69
  375.2 0.0 reduce-scatter.2.cloned.1.call-update
  375.3 96.1 %reduce-scatter.2.cloned.1.call-done = f32[24,768]{1,0:T(8,128)} async-done(((f32[768,768]{1,0:T(8,128)}), f32[24,768]{1,0:T(8,128)}) %reduce-scatter.2.cloned.1.call-update) | async-done | bytes 73744 | tf_op jit(solution)/shard_map/reduce_scatter | solution.py:68
  471.4 0.0 copy-done.1
  (7 shorter events, 0.1 us)
Async XLA Ops:
  6.5 33.9 %copy-start = (bf16[768,128]{1,0:T(8,128)(2,1)S(1)}, bf16[768,128]{1,0:T(8,128)(2,1)}, u32[]{:S(2)}) copy-start(bf16[768,128]{1,0:T(8,128)(2,1)} %param.7) | copy-start | bytes 589828
  11.7 22.2 %all-to-all-start = ((s32[32,2,3]{2,1,0:T(2,128)}), s32[32,2,3]{2,1,0:T(2,128)S(1)}, u32[]{:S(2)}, u32[]{:S(2)}) async-start(s32[32,2,3]{2,1,0:T(2,128)} %bitcast.4), calls=%async_computation | async-start | bytes 65536 | tf_op jit(solution)/shard_map/all_to_all | solution.py:37
  33.9 192.0 %all-to-all-start.1 = ((bf16[32,2,4,128,128]{4,3,2,1,0:T(8,128)(2,1)}), bf16[32,2,4,128,128]{4,3,2,1,0:T(8,128)(2,1)}, u32[]{:S(2)}, u32[]{:S(2)}) async-start(bf16[32,2,4,128,128]{4,3,2,1,0:T(8,128)(2,1)} %bitcast.59), calls=%async_computation.1 | async-start | bytes 16777216 | tf_op jit(solution)/shard_map/all_to_all | solution.py:53
  39.8 431.5 %reduce-scatter.2.cloned.1.call-start = ((), (), s32[]{:S(2)}) async-start(), calls=%async_computation.3 | async-start | bytes 2433024 | tf_op jit(solution)/shard_map/reduce_scatter | solution.py:68
  347.1 124.2 %copy-start.1 = (bf16[768,128]{1,0:T(8,128)(2,1)S(1)}, bf16[768,128]{1,0:T(8,128)(2,1)}, u32[]{:S(2)}) copy-start(bf16[768,128]{1,0:T(8,128)(2,1)} %param.7) | copy-start | bytes 589828
Sparse Core Ops, SparseCore 0:
  375.4 95.9 reduce-scatter.1
where the time goes:
time: 480 us; the launch traced here: 478 us
  waiting for transfers between devices  281 us (59%)
  local copies, waits for them, and re-layouts  113 us (24%)
  matrix products  55.2 us (12%)
  between operations  14.2 us (3%)
  starting transfers between devices  13.4 us (3%)
    all_to_all x1, waiting for transfers between devices, body(): lax.all_to_all(outgoing, 'aux', split_axis=0, concat_axis=0, tiled=True)  184 us
    reduce_scatter x1, waiting for transfers between devices, body(): lax.psum_scatter(lax.dot_general(fitted, fitted, (((1,), (1,)), ((), ()))...  96.1 us
    reshape x1, local copies, waits for them, and re-layouts, body(): fitted.transpose(0, 3, 1, 2, 4)  41 us
    reshape x1, local copies, waits for them, and re-layouts, body(): fitted.astype(jnp.bfloat16)  32.3 us
    dot_general x1, matrix products, body(): lax.dot_general(fitted, fitted, (((1,), (1,)), ((), ())), preferred_eleme...  28.1 us
    unnamed x10, local copies, waits for them, and re-layouts  21.9 us
    dot_general x1, matrix products, body(): jnp.dot(seg_table, half_rows.reshape(aux_nodes * slot_count, -1), preferr...  18.1 us
  transfers between devices with their start and end apart: 3, of which 2 were waited for; matrix products, arithmetic and copies ran while one was open for 3% of the time, Pallas kernels for 0%

commit v1 on v0

--- a/solution.py
+++ b/solution.py
@@ -1,10 +1,324 @@
+import functools
+
 import jax
 import jax.numpy as jnp
 from jax import lax
+from jax.experimental import pallas as pl
+from jax.experimental.pallas import tpu as pltpu
 from jax.sharding import PartitionSpec as P
 
 AUX_DEV = 128
 OCC = 128
+MESH = pl.DeviceIdType.MESH
+NT = (((1,), (1,)), ((), ()))
+
+
+def send_half_blocks(nodes, slots, source, vblock, tags, integrals, coeffs, recv, recv_tags,
+                     half, send_sem, recv_sem, tag_send, tag_recv, own_sem):
+    me = lax.axis_index("aux")
+    barrier = pltpu.get_barrier_semaphore()
+
+    @pl.loop(1, nodes)
+    def _(k):
+        pl.semaphore_signal(
+            barrier, inc=1, device_id={"aux": lax.rem(me + k, nodes)}, device_id_type=MESH
+        )
+
+    def fill(peer):
+        for s in range(slots):
+            block = integrals[source[peer, s]]
+            panel = coeffs[vblock[peer, s]]
+            aux_width, size, inner = block.shape
+            out = jnp.dot(
+                block.reshape(aux_width * size, inner), panel, preferred_element_type=jnp.float32
+            )
+            half[peer, s] = out.astype(jnp.bfloat16).reshape(aux_width, size, panel.shape[1])
+
+    def order(i):
+        return nodes // 2 + (i + 1) // 2 * (1 - 2 * (i % 2))
+
+    def copies(i):
+        k = order(i)
+        peer = lax.rem(me + k, nodes)
+        data = pltpu.make_async_remote_copy(
+            src_ref=half.at[peer], dst_ref=recv.at[me], send_sem=send_sem.at[k],
+            recv_sem=recv_sem.at[k], device_id={"aux": peer}, device_id_type=MESH,
+        )
+        tag = pltpu.make_async_remote_copy(
+            src_ref=tags.at[peer], dst_ref=recv_tags.at[me], send_sem=tag_send.at[k],
+            recv_sem=tag_recv.at[k], device_id={"aux": peer}, device_id_type=MESH,
+        )
+        return data, tag
+
+    fill(lax.rem(me + nodes // 2, nodes))
+    pl.semaphore_wait(barrier, nodes - 1)
+
+    @pl.loop(0, nodes - 1)
+    def _(i):
+        data, tag = copies(i)
+        data.start()
+        tag.start()
+        later = jnp.where(i == nodes - 2, 0, order(i + 1))
+        fill(lax.rem(me + later, nodes))
+
+    own = pltpu.make_async_copy(half.at[me], recv.at[me], own_sem.at[0])
+    own_tag = pltpu.make_async_copy(tags.at[me], recv_tags.at[me], own_sem.at[1])
+    own.start()
+    own_tag.start()
+    own.wait()
+    own_tag.wait()
+
+    @pl.loop(0, nodes - 1)
+    def _(i):
+        data, tag = copies(i)
+        data.wait()
+        tag.wait()
+
+
+def gram(scale, slots, tags, recv, out, total, fitted, head, following, count, mask):
+    nodes, _, aux_width, size, occ = recv.shape
+    owned = head.shape[0]
+    wide = 2 * size
+    groups = out.shape[0] // wide
+    out[...] = jnp.zeros_like(out)
+
+    @pl.loop(0, owned)
+    def _(a):
+        head[a] = 0
+        count[a] = 0
+        mask[a] = 0
+
+    @pl.loop(0, nodes)
+    def _(node):
+        for s in range(slots):
+            a = tags[node, 2 * s]
+            u = tags[node, 2 * s + 1]
+
+            @pl.when(u >= 0)
+            def _():
+                item = node * slots + s
+                following[item] = head[a]
+                head[a] = item
+                count[a] = count[a] + 1
+                mask[a] = mask[a] | (1 << (u // 2))
+
+    @pl.loop(0, owned)
+    def _(a):
+        bits = mask[a]
+        here = [((bits >> i) & 1) == 1 for i in range(groups)]
+        spans = [pl.ds(i * wide, wide) for i in range(groups)]
+
+        @pl.when(bits != 0)
+        def _():
+            for i in range(groups):
+                @pl.when(here[i])
+                def _():
+                    total[spans[i], :] = jnp.zeros((wide, total.shape[1]), jnp.float32)
+
+            def add(_, item):
+                node, s = item // slots, item % slots
+                u = tags[node, 2 * s + 1]
+                rows = pl.ds(pl.multiple_of(u * size, size), size)
+                for p in range(aux_width):
+                    total[rows, pl.ds(p * occ, occ)] += recv[node, s, p].astype(jnp.float32)
+                return following[item]
+
+            lax.fori_loop(0, count[a], add, head[a])
+            for i in range(groups):
+                @pl.when(here[i])
+                def _():
+                    fitted[spans[i], :] = total[spans[i], :].astype(jnp.bfloat16)
+            for i in range(groups):
+                for j in range(groups):
+                    @pl.when(here[i] & here[j])
+                    def _():
+                        out[spans[i], spans[j]] += lax.dot_general(
+                            fitted[spans[i], :], fitted[spans[j], :], NT,
+                            preferred_element_type=jnp.float32,
+                        )
+
+    out[...] = out[...] * scale
+
+
+def exchange(buf, cols, dims, name, coords, sizes, rank_of, landing, send_sem, recv_sem):
+    at = dims.index(name)
+    found = []
+    for step in range(1, sizes[name]):
+        other = lax.rem(coords[name] + step, sizes[name])
+        target = dict(coords)
+        target[name] = other
+        pick = (slice(None),) * at + (other,) + (slice(None),) * (len(dims) - at - 1)
+        found.append(
+            pltpu.make_async_remote_copy(
+                src_ref=buf.at[pick + (slice(None), cols)], dst_ref=landing.at[step - 1],
+                send_sem=send_sem.at[step - 1], recv_sem=recv_sem.at[step - 1],
+                device_id={"aux": rank_of(target)}, device_id_type=MESH,
+            )
+        )
+    return found
+
+
+def gathered(buf, cols, dims, name, coords, landing, copies):
+    at = dims.index(name)
+    pick = (slice(None),) * at + (coords[name],) + (slice(None),) * (len(dims) - at - 1)
+    value = buf[pick + (slice(None), cols)]
+    for step, copy in enumerate(copies):
+        copy.wait()
+        value = value + landing[step]
+    return value
+
+
+ORDERS = (("x", "y", "z"), ("y", "z", "x"), ("z", "x", "y"))
+
+
+def scatter_sum(sizes, part, *refs):
+    own, out, first, landed = refs[:4]
+    lands = refs[4:13]
+    held = refs[13:19]
+    send_sem, recv_sem = refs[19:]
+    me = lax.axis_index("aux")
+    names = ("z", "y", "x", "c")
+    coords = {
+        "c": me % 2, "x": me // 2 % 2, "y": me // 4 % 2, "z": me // 8,
+    }
+
+    def rank_of(c):
+        return ((c["z"] * sizes["y"] + c["y"]) * sizes["x"] + c["x"]) * sizes["c"] + c["c"]
+
+    barrier = pltpu.get_barrier_semaphore()
+    partners = 0
+    for name in names:
+        for step in range(1, sizes[name]):
+            target = dict(coords)
+            target[name] = lax.rem(coords[name] + step, sizes[name])
+            pl.semaphore_signal(
+                barrier, inc=1, device_id={"aux": rank_of(target)}, device_id_type=MESH
+            )
+            partners += 1
+    pl.semaphore_wait(barrier, partners)
+
+    everything = slice(None)
+    copies = exchange(own, everything, names, "c", coords, sizes, rank_of, landed,
+                      send_sem.at[9], recv_sem.at[9])
+    for copy in copies:
+        copy.start()
+    first[...] = gathered(own, everything, names, "c", coords, landed, copies)
+    bufs = [first] * 3
+    left = [list(names[:3]) for _ in range(3)]
+    for stage in range(3):
+        running = []
+        for p in range(3):
+            cols = pl.ds(p * part, part) if stage == 0 else slice(None)
+            lane = stage * 3 + p
+            copies = exchange(bufs[p], cols, left[p], ORDERS[p][stage], coords, sizes, rank_of,
+                              lands[lane], send_sem.at[lane], recv_sem.at[lane])
+            for copy in copies:
+                copy.start()
+            running.append((cols, copies))
+        for p in range(3):
+            cols, copies = running[p]
+            value = gathered(bufs[p], cols, left[p], ORDERS[p][stage], coords,
+                             lands[stage * 3 + p], copies)
+            if stage == 2:
+                out[:, pl.ds(p * part, part)] = value
+            else:
+                bufs[p] = held[stage * 3 + p]
+                bufs[p][...] = value
+            left[p].remove(ORDERS[p][stage])
+
+
+def reduce_scatter(matrix, nodes):
+    rows, columns = matrix.shape
+    sizes = {"z": nodes // 8, "y": 2, "x": 2, "c": 2}
+    height, part = rows // nodes, columns // 3
+    deepest = max(sizes["z"] - 1, 1)
+    lands, held = [], []
+    for stage in range(3):
+        for p in range(3):
+            rest = tuple(sizes[d] for d in ("z", "y", "x") if d not in ORDERS[p][: stage + 1])
+            shape = rest + (height, part)
+            lands.append(pltpu.VMEM((sizes[ORDERS[p][stage]] - 1,) + shape, jnp.float32))
+            if stage < 2:
+                held.append(pltpu.VMEM(shape, jnp.float32))
+    half = (sizes["z"], 2, 2, height, columns)
+    return pl.pallas_call(
+        functools.partial(scatter_sum, sizes, part),
+        out_shape=jax.ShapeDtypeStruct((height, columns), jnp.float32),
+        in_specs=[pl.BlockSpec(memory_space=pltpu.VMEM)],
+        out_specs=pl.BlockSpec(memory_space=pltpu.VMEM),
+        scratch_shapes=[
+            pltpu.VMEM(half, jnp.float32),
+            pltpu.VMEM((1,) + half, jnp.float32),
+            *lands,
+            *held,
+            pltpu.SemaphoreType.DMA((10, deepest)),
+            pltpu.SemaphoreType.DMA((10, deepest)),
+        ],
+        compiler_params=pltpu.CompilerParams(
+            collective_id=1, has_side_effects=True, vmem_limit_bytes=40 * 2**20
+        ),
+    )(matrix.reshape(sizes["z"], 2, 2, 2, height, columns))
+
+
+def fused_body(integrals, block_list, block_count, coeffs):
+    stored, aux_width, size, _ = integrals.shape
+    basis, occ = coeffs.shape
+    nodes = lax.axis_size("aux")
+    owned = AUX_DEV // aux_width
+    slots = max(2, 64 // nodes)
+    positions = jnp.arange(stored, dtype=jnp.int32)
+    owner = jnp.where(positions < block_count[0], block_list[:, 0] // owned, nodes)
+    before = (owner[:, None] == owner[None, :]) & (positions[None, :] < positions[:, None])
+    target = owner * slots + jnp.sum(before.astype(jnp.int32), axis=1)
+    chosen = (target[None, :] == jnp.arange(nodes * slots, dtype=jnp.int32)[:, None]).astype(
+        jnp.int32
+    )
+    fields = jnp.stack(
+        [positions, block_list[:, 2], block_list[:, 0] % owned, block_list[:, 1] + 1], axis=0
+    )
+    picked = jnp.sum(chosen[None] * fields[:, None, :], axis=2)
+    source = picked[0].reshape(nodes, slots)
+    vblock = picked[1].reshape(nodes, slots)
+    tags = jnp.stack([picked[2], picked[3] - 1], axis=1).reshape(nodes, 1, 2 * slots)
+    tags = jnp.pad(tags, ((0, 0), (0, 0), (0, 128 - 2 * slots)))
+    vmem = pl.BlockSpec(memory_space=pltpu.VMEM)
+    smem = pl.BlockSpec(memory_space=pltpu.SMEM)
+    recv, recv_tags = pl.pallas_call(
+        functools.partial(send_half_blocks, nodes, slots),
+        out_shape=(
+            jax.ShapeDtypeStruct((nodes, slots, aux_width, size, occ), jnp.bfloat16),
+            jax.ShapeDtypeStruct((nodes, 1, 128), jnp.int32),
+        ),
+        in_specs=[smem, smem, vmem, vmem, vmem],
+        out_specs=(pl.BlockSpec(memory_space=pl.ANY), vmem),
+        scratch_shapes=[
+            pltpu.VMEM((nodes, slots, aux_width, size, occ), jnp.bfloat16),
+            pltpu.SemaphoreType.DMA((nodes,)),
+            pltpu.SemaphoreType.DMA((nodes,)),
+            pltpu.SemaphoreType.DMA((nodes,)),
+            pltpu.SemaphoreType.DMA((nodes,)),
+            pltpu.SemaphoreType.DMA((2,)),
+        ],
+        compiler_params=pltpu.CompilerParams(
+            collective_id=0, has_side_effects=True, vmem_limit_bytes=40 * 2**20
+        ),
+    )(source, vblock, tags, integrals, coeffs.reshape(basis // size, size, occ))
+    matrix = pl.pallas_call(
+        functools.partial(gram, 1.0 / (AUX_DEV * nodes * OCC), slots),
+        out_shape=jax.ShapeDtypeStruct((basis, basis), jnp.float32),
+        in_specs=[smem, vmem],
+        out_specs=vmem,
+        scratch_shapes=[
+            pltpu.VMEM((basis, aux_width * occ), jnp.float32),
+            pltpu.VMEM((basis, aux_width * occ), jnp.bfloat16),
+            pltpu.SMEM((owned,), jnp.int32),
+            pltpu.SMEM((nodes * slots,), jnp.int32),
+            pltpu.SMEM((owned,), jnp.int32),
+            pltpu.SMEM((owned,), jnp.int32),
+        ],
+        compiler_params=pltpu.CompilerParams(vmem_limit_bytes=40 * 2**20),
+    )(recv_tags.reshape(nodes, 128), recv)
+    return reduce_scatter(matrix, nodes)
 
 
 def body(integrals, block_list, block_count, coeffs):
@@ -83,6 +397,7 @@
         P(("frag", "aux")),
         P("frag", "occ"),
     )
+    simple = mesh.shape["occ"] == 1 and mesh.shape["aux"] % 8 == 0
     return jax.shard_map(
-        body, mesh=mesh, in_specs=placed, out_specs=P(("frag", "aux", "occ"), None), check_vma=False
-    )
+        fused_body if simple else body, mesh=mesh, in_specs=placed, out_specs=P(("frag", "aux", "occ"), None), check_vma=False
+    )

time: 480 us -> 269 us (0.56)
  waiting for transfers between devices: 281 us -> 0 us
  Pallas kernels: 0 us -> 261 us
  local copies, waits for them, and re-layouts: 113 us -> 4.43 us
  matrix products: 55.2 us -> 0 us
  between operations: 14.2 us -> 0.72 us
  starting transfers between devices: 13.4 us -> 0 us
    pallas_call x0 -> x3, Pallas kernels: none -> 261 us  [the longest x1 188 us: fused_body(): pl.pallas_call(functools.partial(send_half_blocks, nodes, slots), out_sha...]
    all_to_all x2 -> x0, waiting for transfers between devices: 184 us -> none  [the longest x1 184 us: body(): lax.all_to_all(outgoing, 'aux', split_axis=0, concat_axis=0, tiled=True)]
    reduce_scatter x1 -> x0, waiting for transfers between devices: 96.1 us -> none  [body(): lax.psum_scatter(lax.dot_general(fitted, fitted, (((1,), (1,)), ((), ()))...]
    reshape x2 -> x1, local copies, waits for them, and re-layouts: 73.3 us -> 0.08 us  [fused_body(): jnp.stack([picked[2], picked[3] - 1], axis=1).reshape(nodes, 1, 2 * slots)]
    dot_general x3 -> x0, matrix products: 55.2 us -> none  [the longest x1 28.1 us: body(): lax.dot_general(fitted, fitted, (((1,), (1,)), ((), ())), preferred_eleme...]
    unnamed x10 -> x5, local copies, waits for them, and re-layouts: 21.9 us -> 4.04 us
    all_to_all x2 -> x0, starting transfers between devices: 13.2 us -> none  [the longest x1 7.3 us: body(): lax.all_to_all(send_tags, 'aux', split_axis=0, concat_axis=0, tiled=True)]
    gather x3 -> x0, local copies, waits for them, and re-layouts: 10.1 us -> none  [the longest x1 7.98 us: body(): padded[source]]
  transfers between devices with their start and end apart: 3 -> 0, of which waited for: 2 -> 0; matrix products, arithmetic and copies ran while one was open for 3% -> 0% of each run, Pallas kernels for 0% -> 0%
where the time goes in v1:
time: 269 us
  Pallas kernels  261 us (97%)
  local copies, waits for them, and re-layouts  4.43 us (2%)
  other arithmetic  3.27 us (1%)
    pallas_call x1, Pallas kernels, fused_body(): pl.pallas_call(functools.partial(send_half_blocks, nodes, slots), out_sha...  188 us
    pallas_call x1, Pallas kernels, reduce_scatter(): pl.pallas_call(functools.partial(scatter_sum, sizes, part), out_shape=jax...  52.9 us
    pallas_call x1, Pallas kernels, fused_body(): pl.pallas_call(functools.partial(gram, 1.0 / (AUX_DEV * nodes * OCC), slo...  20 us

profile of v1, /device:TPU:0, one launch (start us, length us, event | category | flops | bytes accessed | tf_op | source)
XLA Modules:
  0.0 269.0 jit_solution(10979938314690188936)
XLA Ops:
  0.7 0.7 compare_select_fusion.3
  1.3 0.7 and_select_fusion
  2.0 0.8 fusion.2
  2.8 0.2 convert_reduce_fusion
  3.0 0.7 multiply_add_fusion
  3.7 0.1 fusion.1
  3.8 0.1 multiply_reduce_fusion
  3.9 0.1 reshape_squeeze.7.vblock
  4.0 0.1 reshape_squeeze.6.source
  4.2 0.1 copy.9
  4.2 0.1 reshape.165
  4.3 0.0 copy-start
  4.4 2.5 copy-done
  6.8 0.0 copy-start.1
  6.8 0.9 copy-done.1
  7.8 187.6 %shard_map.46 = (bf16[32,2,4,128,128]{4,3,2,1,0:T(8,128)(2,1)S(1)}, s32[32,1,128]{2,1,0:T(1,128)S(1)}) custom-call(s32[32,2]{1,0:T(8,128)S(1)} %reshape_squeeze.6.source, s32[32,2]{1,0:T(8,128)S(1)} %reshape_squeeze.7.vblock, s32[32,1,128]{2,1,0:T(1,128)S(1)} %pad.4.tags, bf16[40,4,128,128]{3,2,1,0:T(8,128)(2,1)S(1)} %copy-done, ...), custom_call_target="tpu_custom_call" | custom-call | tf_op jit(solution)/shard_map/pallas_call | solution.py:286
  195.4 20.0 %shard_map.47 = f32[768,768]{1,0:T(8,128)S(1)} custom-call(s32[32,128]{1,0:T(8,128)S(1)} %bitcast.34, bf16[32,2,4,128,128]{4,3,2,1,0:T(8,128)(2,1)S(1)} %get-tuple-element.8.recv), custom_call_target="tpu_custom_call" | custom-call | tf_op jit(solution)/shard_map/pallas_call | solution.py:306
  215.4 52.9 %shard_map.48 = f32[24,768]{1,0:T(8,128)S(1)} custom-call(f32[4,2,2,2,24,768]{5,4,3,2,1,0:T(8,128)S(1)} %bitcast.32), custom_call_target="tpu_custom_call" | custom-call | tf_op jit(solution)/shard_map/pallas_call | solution.py:244
  268.3 0.6 copy.13
  (5 shorter events, 0.1 us)
Async XLA Ops:
  4.3 2.5 copy-start
  6.8 0.9 copy-start.1

commit v2 on v1

--- a/solution.py
+++ b/solution.py
@@ -34,43 +34,50 @@
             )
             half[peer, s] = out.astype(jnp.bfloat16).reshape(aux_width, size, panel.shape[1])
 
-    def order(i):
-        return nodes // 2 + (i + 1) // 2 * (1 - 2 * (i % 2))
-
-    def copies(i):
-        k = order(i)
-        peer = lax.rem(me + k, nodes)
+    half_nodes = nodes // 2
+    side, place = me // half_nodes, lax.rem(me, half_nodes)
+
+    def peer_of(i):
+        other = lax.rem(side + 1 - i % 2, 2)
+        return other * half_nodes + lax.rem(place + i // 2, half_nodes)
+
+    def copies(peer, landed):
         data = pltpu.make_async_remote_copy(
-            src_ref=half.at[peer], dst_ref=recv.at[me], send_sem=send_sem.at[k],
-            recv_sem=recv_sem.at[k], device_id={"aux": peer}, device_id_type=MESH,
+            src_ref=half.at[peer], dst_ref=recv.at[me], send_sem=send_sem.at[peer],
+            recv_sem=recv_sem.at[landed], device_id={"aux": peer}, device_id_type=MESH,
         )
         tag = pltpu.make_async_remote_copy(
-            src_ref=tags.at[peer], dst_ref=recv_tags.at[me], send_sem=tag_send.at[k],
-            recv_sem=tag_recv.at[k], device_id={"aux": peer}, device_id_type=MESH,
+            src_ref=tags.at[peer], dst_ref=recv_tags.at[me], send_sem=tag_send.at[peer],
+            recv_sem=tag_recv.at[landed], device_id={"aux": peer}, device_id_type=MESH,
         )
         return data, tag
 
-    fill(lax.rem(me + nodes // 2, nodes))
-    pl.semaphore_wait(barrier, nodes - 1)
-
-    @pl.loop(0, nodes - 1)
-    def _(i):
-        data, tag = copies(i)
+    def send(i):
+        peer = peer_of(i)
+        fill(peer)
+        data, tag = copies(peer, me)
         data.start()
         tag.start()
-        later = jnp.where(i == nodes - 2, 0, order(i + 1))
-        fill(lax.rem(me + later, nodes))
-
+
+    pl.semaphore_wait(barrier, nodes - 1)
+    send(0)
+    fill(me)
     own = pltpu.make_async_copy(half.at[me], recv.at[me], own_sem.at[0])
     own_tag = pltpu.make_async_copy(tags.at[me], recv_tags.at[me], own_sem.at[1])
     own.start()
     own_tag.start()
+
+    @pl.loop(2, nodes)
+    def _(i):
+        send(i)
+
     own.wait()
     own_tag.wait()
 
-    @pl.loop(0, nodes - 1)
-    def _(i):
-        data, tag = copies(i)
+    @pl.loop(1, nodes)
+    def _(k):
+        peer = lax.rem(me + k, nodes)
+        data, tag = copies(peer, peer)
         data.wait()
         tag.wait()
 

time: 269 us -> 265 us (0.985); the launches traced: 269 us -> 268 us
    pallas_call x1, Pallas kernels: 188 us -> 207 us  [fused_body(): pl.pallas_call(functools.partial(send_half_blocks, nodes, slots), out_sha...]
    pallas_call x1, Pallas kernels: 52.9 us -> 37 us  [reduce_scatter(): pl.pallas_call(functools.partial(scatter_sum, sizes, part), out_shape=jax...]
    pallas_call x1, Pallas kernels: 20 us -> 15.8 us  [fused_body(): pl.pallas_call(functools.partial(gram, 1.0 / (AUX_DEV * nodes * OCC), slo...]
where the time goes in v2:
time: 265 us; the launch traced here: 268 us
  Pallas kernels  260 us (98%)
  local copies, waits for them, and re-layouts  4.43 us (2%)
  other arithmetic  3.27 us (1%)
    pallas_call x1, Pallas kernels, fused_body(): pl.pallas_call(functools.partial(send_half_blocks, nodes, slots), out_sha...  207 us
    pallas_call x1, Pallas kernels, reduce_scatter(): pl.pallas_call(functools.partial(scatter_sum, sizes, part), out_shape=jax...  37 us
    pallas_call x1, Pallas kernels, fused_body(): pl.pallas_call(functools.partial(gram, 1.0 / (AUX_DEV * nodes * OCC), slo...  15.8 us

profile of v2, /device:TPU:0, one launch (start us, length us, event | category | flops | bytes accessed | tf_op | source)
XLA Modules:
  0.0 268.0 jit_solution(14451671091497545102)
XLA Ops:
  0.7 0.7 compare_select_fusion.3
  1.3 0.7 and_select_fusion
  2.0 0.8 fusion.2
  2.8 0.2 convert_reduce_fusion
  3.0 0.7 multiply_add_fusion
  3.7 0.1 fusion.1
  3.8 0.1 multiply_reduce_fusion
  3.9 0.1 reshape_squeeze.7.vblock
  4.0 0.1 reshape_squeeze.6.source
  4.2 0.1 copy.9
  4.2 0.1 reshape.165
  4.3 0.0 copy-start
  4.4 2.5 copy-done
  6.8 0.0 copy-start.1
  6.8 0.9 copy-done.1
  7.8 206.7 %shard_map.46 = (bf16[32,2,4,128,128]{4,3,2,1,0:T(8,128)(2,1)S(1)}, s32[32,1,128]{2,1,0:T(1,128)S(1)}) custom-call(s32[32,2]{1,0:T(8,128)S(1)} %reshape_squeeze.6.source, s32[32,2]{1,0:T(8,128)S(1)} %reshape_squeeze.7.vblock, s32[32,1,128]{2,1,0:T(1,128)S(1)} %pad.4.tags, bf16[40,4,128,128]{3,2,1,0:T(8,128)(2,1)S(1)} %copy-done, ...), custom_call_target="tpu_custom_call" | custom-call | tf_op jit(solution)/shard_map/pallas_call | solution.py:293
  214.5 15.8 %shard_map.47 = f32[768,768]{1,0:T(8,128)S(1)} custom-call(s32[32,128]{1,0:T(8,128)S(1)} %bitcast.34, bf16[32,2,4,128,128]{4,3,2,1,0:T(8,128)(2,1)S(1)} %get-tuple-element.8.recv), custom_call_target="tpu_custom_call" | custom-call | tf_op jit(solution)/shard_map/pallas_call | solution.py:313
  230.3 37.0 %shard_map.48 = f32[24,768]{1,0:T(8,128)S(1)} custom-call(f32[4,2,2,2,24,768]{5,4,3,2,1,0:T(8,128)S(1)} %bitcast.32), custom_call_target="tpu_custom_call" | custom-call | tf_op jit(solution)/shard_map/pallas_call | solution.py:251
  267.3 0.6 copy.13
  (5 shorter events, 0.1 us)
Async XLA Ops:
  4.3 2.5 copy-start
  6.8 0.9 copy-start.1

commit v3 on v2

--- a/solution.py
+++ b/solution.py
@@ -34,12 +34,14 @@
             )
             half[peer, s] = out.astype(jnp.bfloat16).reshape(aux_width, size, panel.shape[1])
 
-    half_nodes = nodes // 2
-    side, place = me // half_nodes, lax.rem(me, half_nodes)
-
     def peer_of(i):
-        other = lax.rem(side + 1 - i % 2, 2)
-        return other * half_nodes + lax.rem(place + i // 2, half_nodes)
+        pair = i // 2
+        flips = (1 - i % 2) * (nodes // 2) + pair % 2 * (nodes // 4) + pair // 2
+        peer, bit = 0, 1
+        while bit < nodes:
+            peer = peer + (me // bit + flips // bit) % 2 * bit
+            bit *= 2
+        return peer
 
     def copies(peer, landed):
         data = pltpu.make_async_remote_copy(
@@ -95,6 +97,10 @@
         count[a] = 0
         mask[a] = 0
 
+    @pl.loop(0, nodes * slots)
+    def _(item):
+        following[item] = 0
+
     @pl.loop(0, nodes)
     def _(node):
         for s in range(slots):
@@ -115,7 +121,37 @@
         here = [((bits >> i) & 1) == 1 for i in range(groups)]
         spans = [pl.ds(i * wide, wide) for i in range(groups)]
 
-        @pl.when(bits != 0)
+        members = count[a]
+        item = head[a]
+        second = following[item]
+        row = tags[item // slots, 2 * (item % slots) + 1]
+        row_second = tags[second // slots, 2 * (second % slots) + 1]
+        two = (members == 2) & (row != row_second)
+
+        def panel(which):
+            node, s = which // slots, which % slots
+            return jnp.concatenate([recv[node, s, p] for p in range(aux_width)], axis=1)
+
+        def span(u):
+            return pl.ds(pl.multiple_of(u * size, size), size)
+
+        @pl.when(members == 1)
+        def _():
+            x = panel(item)
+            out[span(row), span(row)] += lax.dot_general(
+                x, x, NT, preferred_element_type=jnp.float32
+            )
+
+        @pl.when(two)
+        def _():
+            x = jnp.concatenate([panel(item), panel(second)], axis=0)
+            product = lax.dot_general(x, x, NT, preferred_element_type=jnp.float32)
+            out[span(row), span(row)] += product[:size, :size]
+            out[span(row), span(row_second)] += product[:size, size:]
+            out[span(row_second), span(row)] += product[size:, :size]
+            out[span(row_second), span(row_second)] += product[size:, size:]
+
+        @pl.when((members > 1) & jnp.logical_not(two))
         def _():
             for i in range(groups):
                 @pl.when(here[i])
@@ -178,11 +214,11 @@
 ORDERS = (("x", "y", "z"), ("y", "z", "x"), ("z", "x", "y"))
 
 
-def scatter_sum(sizes, part, *refs):
-    own, out, first, landed = refs[:4]
-    lands = refs[4:13]
-    held = refs[13:19]
-    send_sem, recv_sem = refs[19:]
+def scatter_sum(sizes, starts, *refs):
+    own, out = refs[:2]
+    lands = refs[2:14]
+    held = refs[14:23]
+    send_sem, recv_sem = refs[23:]
     me = lax.axis_index("aux")
     names = ("z", "y", "x", "c")
     coords = {
@@ -204,62 +240,61 @@
             partners += 1
     pl.semaphore_wait(barrier, partners)
 
-    everything = slice(None)
-    copies = exchange(own, everything, names, "c", coords, sizes, rank_of, landed,
-                      send_sem.at[9], recv_sem.at[9])
-    for copy in copies:
-        copy.start()
-    first[...] = gathered(own, everything, names, "c", coords, landed, copies)
-    bufs = [first] * 3
-    left = [list(names[:3]) for _ in range(3)]
-    for stage in range(3):
-        running = []
-        for p in range(3):
-            cols = pl.ds(p * part, part) if stage == 0 else slice(None)
-            lane = stage * 3 + p
-            copies = exchange(bufs[p], cols, left[p], ORDERS[p][stage], coords, sizes, rank_of,
-                              lands[lane], send_sem.at[lane], recv_sem.at[lane])
-            for copy in copies:
-                copy.start()
-            running.append((cols, copies))
+    orders = [("c",) + order for order in ORDERS]
+    bufs = [own] * 3
+    left = [list(names) for _ in range(3)]
+    spans = [pl.ds(starts[p], starts[p + 1] - starts[p]) for p in range(3)]
+
+    def start(p, stage):
+        cols = spans[p] if stage == 0 else slice(None)
+        lane = stage * 3 + p
+        copies = exchange(bufs[p], cols, left[p], orders[p][stage], coords, sizes, rank_of,
+                          lands[lane], send_sem.at[lane], recv_sem.at[lane])
+        for copy in copies:
+            copy.start()
+        return cols, copies
+
+    running = [start(p, 0) for p in range(3)]
+    for stage in range(4):
         for p in range(3):
             cols, copies = running[p]
-            value = gathered(bufs[p], cols, left[p], ORDERS[p][stage], coords,
+            value = gathered(bufs[p], cols, left[p], orders[p][stage], coords,
                              lands[stage * 3 + p], copies)
-            if stage == 2:
-                out[:, pl.ds(p * part, part)] = value
-            else:
-                bufs[p] = held[stage * 3 + p]
-                bufs[p][...] = value
-            left[p].remove(ORDERS[p][stage])
+            if stage == 3:
+                out[:, spans[p]] = value
+                continue
+            bufs[p] = held[stage * 3 + p]
+            bufs[p][...] = value
+            left[p].remove(orders[p][stage])
+            running[p] = start(p, stage + 1)
 
 
 def reduce_scatter(matrix, nodes):
     rows, columns = matrix.shape
     sizes = {"z": nodes // 8, "y": 2, "x": 2, "c": 2}
-    height, part = rows // nodes, columns // 3
+    height = rows // nodes
+    starts = (0, columns // 2, columns // 6 * 5, columns)
     deepest = max(sizes["z"] - 1, 1)
     lands, held = [], []
-    for stage in range(3):
+    for stage in range(4):
         for p in range(3):
-            rest = tuple(sizes[d] for d in ("z", "y", "x") if d not in ORDERS[p][: stage + 1])
-            shape = rest + (height, part)
-            lands.append(pltpu.VMEM((sizes[ORDERS[p][stage]] - 1,) + shape, jnp.float32))
-            if stage < 2:
+            done = ("c",) + ORDERS[p][:stage]
+            rest = tuple(sizes[d] for d in ("z", "y", "x") if d not in done)
+            shape = rest + (height, starts[p + 1] - starts[p])
+            axis = done[-1]
+            lands.append(pltpu.VMEM((sizes[axis] - 1,) + shape, jnp.float32))
+            if stage < 3:
                 held.append(pltpu.VMEM(shape, jnp.float32))
-    half = (sizes["z"], 2, 2, height, columns)
     return pl.pallas_call(
-        functools.partial(scatter_sum, sizes, part),
+        functools.partial(scatter_sum, sizes, starts),
         out_shape=jax.ShapeDtypeStruct((height, columns), jnp.float32),
         in_specs=[pl.BlockSpec(memory_space=pltpu.VMEM)],
         out_specs=pl.BlockSpec(memory_space=pltpu.VMEM),
         scratch_shapes=[
-            pltpu.VMEM(half, jnp.float32),
-            pltpu.VMEM((1,) + half, jnp.float32),
             *lands,
             *held,
-            pltpu.SemaphoreType.DMA((10, deepest)),
-            pltpu.SemaphoreType.DMA((10, deepest)),
+            pltpu.SemaphoreType.DMA((12, deepest)),
+            pltpu.SemaphoreType.DMA((12, deepest)),
         ],
         compiler_params=pltpu.CompilerParams(
             collective_id=1, has_side_effects=True, vmem_limit_bytes=40 * 2**20
@@ -404,7 +439,7 @@
         P(("frag", "aux")),
         P("frag", "occ"),
     )
-    simple = mesh.shape["occ"] == 1 and mesh.shape["aux"] % 8 == 0
+    simple = mesh.shape["occ"] == 1 and mesh.shape["aux"] in (8, 16, 32, 64)
     return jax.shard_map(
         fused_body if simple else body, mesh=mesh, in_specs=placed, out_specs=P(("frag", "aux", "occ"), None), check_vma=False
     )

time: 265 us -> 254 us (0.958); the launches traced: 268 us -> 253 us
  Pallas kernels: 260 us -> 245 us
    pallas_call x1, Pallas kernels: 207 us -> 192 us  [fused_body(): pl.pallas_call(functools.partial(send_half_blocks, nodes, slots), out_sha...]
where the time goes in v3:
time: 254 us; the launch traced here: 253 us
  Pallas kernels  245 us (96%)
  local copies, waits for them, and re-layouts  4.43 us (2%)
  other arithmetic  3.27 us (1%)
    pallas_call x1, Pallas kernels, fused_body(): pl.pallas_call(functools.partial(send_half_blocks, nodes, slots), out_sha...  192 us
    pallas_call x1, Pallas kernels, reduce_scatter(): pl.pallas_call(functools.partial(scatter_sum, sizes, starts), out_shape=j...  37.3 us
    pallas_call x1, Pallas kernels, fused_body(): pl.pallas_call(functools.partial(gram, 1.0 / (AUX_DEV * nodes * OCC), slo...  16 us

profile of v3, /device:TPU:0, one launch (start us, length us, event | category | flops | bytes accessed | tf_op | source)
XLA Modules:
  0.0 253.2 jit_solution(2899972033093794697)
XLA Ops:
  0.7 0.7 compare_select_fusion.3
  1.3 0.7 and_select_fusion
  2.0 0.8 fusion.2
  2.8 0.2 convert_reduce_fusion
  3.0 0.7 multiply_add_fusion
  3.7 0.1 fusion.1
  3.8 0.1 multiply_reduce_fusion
  3.9 0.1 reshape_squeeze.7.vblock
  4.0 0.1 reshape_squeeze.6.source
  4.2 0.1 copy.9
  4.2 0.1 reshape.165
  4.3 0.0 copy-start
  4.4 2.5 copy-done
  6.8 0.0 copy-start.1
  6.8 0.9 copy-done.1
  7.8 191.5 %shard_map.46 = (bf16[32,2,4,128,128]{4,3,2,1,0:T(8,128)(2,1)S(1)}, s32[32,1,128]{2,1,0:T(1,128)S(1)}) custom-call(s32[32,2]{1,0:T(8,128)S(1)} %reshape_squeeze.6.source, s32[32,2]{1,0:T(8,128)S(1)} %reshape_squeeze.7.vblock, s32[32,1,128]{2,1,0:T(1,128)S(1)} %pad.4.tags, bf16[40,4,128,128]{3,2,1,0:T(8,128)(2,1)S(1)} %copy-done, ...), custom_call_target="tpu_custom_call" | custom-call | tf_op jit(solution)/shard_map/pallas_call | solution.py:328
  199.3 16.0 %shard_map.47 = f32[768,768]{1,0:T(8,128)S(1)} custom-call(s32[32,128]{1,0:T(8,128)S(1)} %bitcast.34, bf16[32,2,4,128,128]{4,3,2,1,0:T(8,128)(2,1)S(1)} %get-tuple-element.8.recv), custom_call_target="tpu_custom_call" | custom-call | tf_op jit(solution)/shard_map/pallas_call | solution.py:348
  215.3 37.3 %shard_map.48 = f32[24,768]{1,0:T(8,128)S(1)} custom-call(f32[4,2,2,2,24,768]{5,4,3,2,1,0:T(8,128)S(1)} %bitcast.32), custom_call_target="tpu_custom_call" | custom-call | tf_op jit(solution)/shard_map/pallas_call | solution.py:288
  252.6 0.6 copy.13
  (5 shorter events, 0.1 us)
Async XLA Ops:
  4.3 2.5 copy-start
  6.8 0.9 copy-start.1

commit v4 on v3

--- a/solution.py
+++ b/solution.py
@@ -84,22 +84,19 @@
         tag.wait()
 
 
-def gram(scale, slots, tags, recv, out, total, fitted, head, following, count, mask):
+def gram(scale, slots, tags, recv, out, total, fitted, head, following, count, distinct, rows):
     nodes, _, aux_width, size, occ = recv.shape
-    owned = head.shape[0]
-    wide = 2 * size
-    groups = out.shape[0] // wide
+    groups = out.shape[0] // size
+    owned = distinct.shape[0]
     out[...] = jnp.zeros_like(out)
 
     @pl.loop(0, owned)
     def _(a):
-        head[a] = 0
-        count[a] = 0
-        mask[a] = 0
-
-    @pl.loop(0, nodes * slots)
-    def _(item):
-        following[item] = 0
+        distinct[a] = 0
+        for u in range(groups):
+            count[a * groups + u] = 0
+            head[a * groups + u] = 0
+            rows[a * groups + u] = 0
 
     @pl.loop(0, nodes)
     def _(node):
@@ -110,75 +107,89 @@
             @pl.when(u >= 0)
             def _():
                 item = node * slots + s
-                following[item] = head[a]
-                head[a] = item
-                count[a] = count[a] + 1
-                mask[a] = mask[a] | (1 << (u // 2))
+                segment = a * groups + u
+                seen = count[segment]
+
+                @pl.when(seen == 0)
+                def _():
+                    rows[a * groups + distinct[a]] = u
+                    distinct[a] = distinct[a] + 1
+
+                following[item] = head[segment]
+                head[segment] = item
+                count[segment] = seen + 1
+
+    def panel(which):
+        node, s = which // slots, which % slots
+        return jnp.concatenate([recv[node, s, p] for p in range(aux_width)], axis=1)
+
+    def span(u):
+        return pl.ds(pl.multiple_of(u * size, size), size)
 
     @pl.loop(0, owned)
     def _(a):
-        bits = mask[a]
-        here = [((bits >> i) & 1) == 1 for i in range(groups)]
-        spans = [pl.ds(i * wide, wide) for i in range(groups)]
-
-        members = count[a]
-        item = head[a]
-        second = following[item]
-        row = tags[item // slots, 2 * (item % slots) + 1]
-        row_second = tags[second // slots, 2 * (second % slots) + 1]
-        two = (members == 2) & (row != row_second)
-
-        def panel(which):
-            node, s = which // slots, which % slots
-            return jnp.concatenate([recv[node, s, p] for p in range(aux_width)], axis=1)
-
-        def span(u):
-            return pl.ds(pl.multiple_of(u * size, size), size)
-
-        @pl.when(members == 1)
+        present = distinct[a]
+        base = a * groups
+        first, second = rows[base], rows[base + 1]
+        once = (count[base + first] == 1) & ((present < 2) | (count[base + second] == 1))
+        simple = once & (present < 3)
+
+        @pl.when(simple & (present == 1))
         def _():
-            x = panel(item)
-            out[span(row), span(row)] += lax.dot_general(
+            x = panel(head[base + first])
+            out[span(first), span(first)] += lax.dot_general(
                 x, x, NT, preferred_element_type=jnp.float32
             )
 
-        @pl.when(two)
+        @pl.when(simple & (present == 2))
         def _():
-            x = jnp.concatenate([panel(item), panel(second)], axis=0)
+            x = jnp.concatenate(
+                [panel(head[base + first]), panel(head[base + second])], axis=0
+            )
             product = lax.dot_general(x, x, NT, preferred_element_type=jnp.float32)
-            out[span(row), span(row)] += product[:size, :size]
-            out[span(row), span(row_second)] += product[:size, size:]
-            out[span(row_second), span(row)] += product[size:, :size]
-            out[span(row_second), span(row_second)] += product[size:, size:]
-
-        @pl.when((members > 1) & jnp.logical_not(two))
+            out[span(first), span(first)] += product[:size, :size]
+            out[span(first), span(second)] += product[:size, size:]
+            out[span(second), span(first)] += product[size:, :size]
+            out[span(second), span(second)] += product[size:, size:]
+
+        @pl.when((present > 0) & jnp.logical_not(simple))
         def _():
-            for i in range(groups):
-                @pl.when(here[i])
+            @pl.loop(0, present)
+            def _(i):
+                segment = base + rows[base + i]
+                item = head[segment]
+                members = count[segment]
+
+                @pl.when(members == 1)
                 def _():
-                    total[spans[i], :] = jnp.zeros((wide, total.shape[1]), jnp.float32)
-
-            def add(_, item):
-                node, s = item // slots, item % slots
-                u = tags[node, 2 * s + 1]
-                rows = pl.ds(pl.multiple_of(u * size, size), size)
-                for p in range(aux_width):
-                    total[rows, pl.ds(p * occ, occ)] += recv[node, s, p].astype(jnp.float32)
-                return following[item]
-
-            lax.fori_loop(0, count[a], add, head[a])
-            for i in range(groups):
-                @pl.when(here[i])
+                    fitted[span(i), :] = panel(item)
+
+                @pl.when(members > 1)
                 def _():
-                    fitted[spans[i], :] = total[spans[i], :].astype(jnp.bfloat16)
-            for i in range(groups):
-                for j in range(groups):
-                    @pl.when(here[i] & here[j])
-                    def _():
-                        out[spans[i], spans[j]] += lax.dot_general(
-                            fitted[spans[i], :], fitted[spans[j], :], NT,
+                    total[...] = panel(item).astype(jnp.float32)
+
+                    def add(_, item):
+                        total[...] += panel(item).astype(jnp.float32)
+                        return following[item]
+
+                    lax.fori_loop(1, members, add, following[item])
+                    fitted[span(i), :] = total[...].astype(jnp.bfloat16)
+
+            for k in range(1, groups + 1):
+                @pl.when(present == k)
+                def _():
+                    for low in range(0, k, 2):
+                        high = min(low + 2, k)
+                        product = lax.dot_general(
+                            fitted[low * size : high * size, :], fitted[: k * size, :], NT,
                             preferred_element_type=jnp.float32,
                         )
+                        for i in range(low, high):
+                            for j in range(k):
+                                out[span(rows[base + i]), span(rows[base + j])] += product[
+                                    (i - low) * size : (i - low + 1) * size,
+                                    j * size : (j + 1) * size,
+                                ]
 
     out[...] = out[...] * scale
 
@@ -309,14 +320,15 @@
     owned = AUX_DEV // aux_width
     slots = max(2, 64 // nodes)
     positions = jnp.arange(stored, dtype=jnp.int32)
-    owner = jnp.where(positions < block_count[0], block_list[:, 0] // owned, nodes)
+    slab = lax.div(block_list[:, 0], jnp.int32(owned))
+    owner = jnp.where(positions < block_count[0], slab, nodes)
     before = (owner[:, None] == owner[None, :]) & (positions[None, :] < positions[:, None])
     target = owner * slots + jnp.sum(before.astype(jnp.int32), axis=1)
     chosen = (target[None, :] == jnp.arange(nodes * slots, dtype=jnp.int32)[:, None]).astype(
         jnp.int32
     )
     fields = jnp.stack(
-        [positions, block_list[:, 2], block_list[:, 0] % owned, block_list[:, 1] + 1], axis=0
+        [positions, block_list[:, 2], block_list[:, 0] - slab * owned, block_list[:, 1] + 1], axis=0
     )
     picked = jnp.sum(chosen[None] * fields[:, None, :], axis=2)
     source = picked[0].reshape(nodes, slots)
@@ -351,12 +363,13 @@
         in_specs=[smem, vmem],
         out_specs=vmem,
         scratch_shapes=[
-            pltpu.VMEM((basis, aux_width * occ), jnp.float32),
+            pltpu.VMEM((size, aux_width * occ), jnp.float32),
             pltpu.VMEM((basis, aux_width * occ), jnp.bfloat16),
+            pltpu.SMEM((owned * (basis // size),), jnp.int32),
+            pltpu.SMEM((nodes * slots,), jnp.int32),
+            pltpu.SMEM((owned * (basis // size),), jnp.int32),
             pltpu.SMEM((owned,), jnp.int32),
-            pltpu.SMEM((nodes * slots,), jnp.int32),
-            pltpu.SMEM((owned,), jnp.int32),
-            pltpu.SMEM((owned,), jnp.int32),
+            pltpu.SMEM((owned * (basis // size),), jnp.int32),
         ],
         compiler_params=pltpu.CompilerParams(vmem_limit_bytes=40 * 2**20),
     )(recv_tags.reshape(nodes, 128), recv)

time: 254 us -> 236 us (0.929)
  Pallas kernels: 245 us -> 228 us
    pallas_call x1, Pallas kernels: 37.3 us -> 27.6 us  [reduce_scatter(): pl.pallas_call(functools.partial(scatter_sum, sizes, starts), out_shape=j...]
    pallas_call x1, Pallas kernels: 16 us -> 8.48 us  [fused_body(): pl.pallas_call(functools.partial(gram, 1.0 / (AUX_DEV * nodes * OCC), slo...]
where the time goes in v4:
time: 236 us
  Pallas kernels  228 us (97%)
  local copies, waits for them, and re-layouts  4.43 us (2%)
  other arithmetic  3.27 us (1%)
    pallas_call x1, Pallas kernels, fused_body(): pl.pallas_call(functools.partial(send_half_blocks, nodes, slots), out_sha...  192 us
    pallas_call x1, Pallas kernels, reduce_scatter(): pl.pallas_call(functools.partial(scatter_sum, sizes, starts), out_shape=j...  27.6 us
    pallas_call x1, Pallas kernels, fused_body(): pl.pallas_call(functools.partial(gram, 1.0 / (AUX_DEV * nodes * OCC), slo...  8.48 us

profile of v4, /device:TPU:0, one launch (start us, length us, event | category | flops | bytes accessed | tf_op | source)
XLA Modules:
  0.0 236.0 jit_solution(3596413460732240043)
XLA Ops:
  0.7 0.7 compare_select_fusion.7
  1.3 0.7 fusion.7
  2.0 0.8 fusion.2
  2.8 0.2 convert_reduce_fusion
  3.0 0.7 multiply_add_fusion
  3.7 0.1 fusion.1
  3.8 0.1 multiply_reduce_fusion
  3.9 0.1 reshape_squeeze.7.vblock
  4.0 0.1 reshape_squeeze.6.source
  4.1 0.1 copy.9
  4.2 0.1 reshape.139
  4.3 0.0 copy-start
  4.4 2.5 %copy-done = bf16[40,4,128,128]{3,2,1,0:T(8,128)(2,1)S(1)} copy-done((bf16[40,4,128,128]{3,2,1,0:T(8,128)(2,1)S(1)}, bf16[40,4,128,128]{3,2,1,0:T(8,128)(2,1)}, u32[]{:S(2)}) %copy-start) | copy-done | bytes 5242904
  6.8 0.0 copy-start.1
  6.8 0.9 copy-done.1
  7.8 191.5 %shard_map.46 = (bf16[32,2,4,128,128]{4,3,2,1,0:T(8,128)(2,1)S(1)}, s32[32,1,128]{2,1,0:T(1,128)S(1)}) custom-call(s32[32,2]{1,0:T(8,128)S(1)} %reshape_squeeze.6.source, s32[32,2]{1,0:T(8,128)S(1)} %reshape_squeeze.7.vblock, s32[32,1,128]{2,1,0:T(1,128)S(1)} %pad.4.tags, bf16[40,4,128,128]{3,2,1,0:T(8,128)(2,1)S(1)} %copy-done, ...), custom_call_target="tpu_custom_call" | custom-call | tf_op jit(solution)/shard_map/pallas_call | solution.py:340
  199.3 8.5 %shard_map.47 = f32[768,768]{1,0:T(8,128)S(1)} custom-call(s32[32,128]{1,0:T(8,128)S(1)} %bitcast.26, bf16[32,2,4,128,128]{4,3,2,1,0:T(8,128)(2,1)S(1)} %get-tuple-element.8.recv), custom_call_target="tpu_custom_call" | custom-call | tf_op jit(solution)/shard_map/pallas_call | solution.py:360
  207.8 27.6 %shard_map.48 = f32[24,768]{1,0:T(8,128)S(1)} custom-call(f32[4,2,2,2,24,768]{5,4,3,2,1,0:T(8,128)S(1)} %bitcast.24), custom_call_target="tpu_custom_call" | custom-call | tf_op jit(solution)/shard_map/pallas_call | solution.py:299
  235.4 0.6 copy.13
  (5 shorter events, 0.1 us)
Async XLA Ops:
  4.3 2.5 %copy-start = (bf16[40,4,128,128]{3,2,1,0:T(8,128)(2,1)S(1)}, bf16[40,4,128,128]{3,2,1,0:T(8,128)(2,1)}, u32[]{:S(2)}) copy-start(bf16[40,4,128,128]{3,2,1,0:T(8,128)(2,1)} %integrals.1) | copy-start | bytes 15728644
  6.8 0.9 copy-start.1

commit v5 on v4

--- a/solution.py
+++ b/solution.py
@@ -36,7 +36,8 @@
 
     def peer_of(i):
         pair = i // 2
-        flips = (1 - i % 2) * (nodes // 2) + pair % 2 * (nodes // 4) + pair // 2
+        flips = (1 - i % 2) * (nodes // 2) + pair % 2 * (nodes // 4)
+        flips = flips + (nodes // 4 - pair // 2) % (nodes // 4)
         peer, bit = 0, 1
         while bit < nodes:
             peer = peer + (me // bit + flips // bit) % 2 * bit
@@ -57,12 +58,16 @@
     def send(i):
         peer = peer_of(i)
         fill(peer)
+        post(peer)
+
+    def post(peer):
         data, tag = copies(peer, me)
         data.start()
         tag.start()
 
+    fill(peer_of(0))
     pl.semaphore_wait(barrier, nodes - 1)
-    send(0)
+    post(peer_of(0))
     fill(me)
     own = pltpu.make_async_copy(half.at[me], recv.at[me], own_sem.at[0])
     own_tag = pltpu.make_async_copy(tags.at[me], recv_tags.at[me], own_sem.at[1])

time: 236 us -> 234 us (level)
  Pallas kernels: 228 us -> 225 us
    pallas_call x1, Pallas kernels: 192 us -> 186 us  [fused_body(): pl.pallas_call(functools.partial(send_half_blocks, nodes, slots), out_sha...]
    pallas_call x1, Pallas kernels: 27.6 us -> 30.5 us  [reduce_scatter(): pl.pallas_call(functools.partial(scatter_sum, sizes, starts), out_shape=j...]
where the time goes in v5:
time: 234 us
  Pallas kernels  225 us (96%)
  local copies, waits for them, and re-layouts  4.43 us (2%)
  other arithmetic  3.27 us (1%)
    pallas_call x1, Pallas kernels, fused_body(): pl.pallas_call(functools.partial(send_half_blocks, nodes, slots), out_sha...  186 us
    pallas_call x1, Pallas kernels, reduce_scatter(): pl.pallas_call(functools.partial(scatter_sum, sizes, starts), out_shape=j...  30.5 us
    pallas_call x1, Pallas kernels, fused_body(): pl.pallas_call(functools.partial(gram, 1.0 / (AUX_DEV * nodes * OCC), slo...  9.19 us

profile of v5, /device:TPU:0, one launch (start us, length us, event | category | flops | bytes accessed | tf_op | source)
XLA Modules:
  0.0 233.7 jit_solution(18434439877769689445)
XLA Ops:
  0.7 0.7 compare_select_fusion.7
  1.3 0.7 fusion.7
  2.0 0.8 fusion.2
  2.8 0.2 convert_reduce_fusion
  3.0 0.7 multiply_add_fusion
  3.7 0.1 fusion.1
  3.8 0.1 multiply_reduce_fusion
  3.9 0.1 reshape_squeeze.7.vblock
  4.0 0.1 reshape_squeeze.6.source
  4.1 0.1 copy.9
  4.2 0.1 reshape.139
  4.3 0.0 copy-start
  4.4 2.5 %copy-done = bf16[40,4,128,128]{3,2,1,0:T(8,128)(2,1)S(1)} copy-done((bf16[40,4,128,128]{3,2,1,0:T(8,128)(2,1)S(1)}, bf16[40,4,128,128]{3,2,1,0:T(8,128)(2,1)}, u32[]{:S(2)}) %copy-start) | copy-done | bytes 5242904
  6.8 0.0 copy-start.1
  6.8 0.9 copy-done.1
  7.8 185.6 %shard_map.46 = (bf16[32,2,4,128,128]{4,3,2,1,0:T(8,128)(2,1)S(1)}, s32[32,1,128]{2,1,0:T(1,128)S(1)}) custom-call(s32[32,2]{1,0:T(8,128)S(1)} %reshape_squeeze.6.source, s32[32,2]{1,0:T(8,128)S(1)} %reshape_squeeze.7.vblock, s32[32,1,128]{2,1,0:T(1,128)S(1)} %pad.4.tags, bf16[40,4,128,128]{3,2,1,0:T(8,128)(2,1)S(1)} %copy-done, ...), custom_call_target="tpu_custom_call" | custom-call | tf_op jit(solution)/shard_map/pallas_call | solution.py:345
  193.4 9.2 %shard_map.47 = f32[768,768]{1,0:T(8,128)S(1)} custom-call(s32[32,128]{1,0:T(8,128)S(1)} %bitcast.26, bf16[32,2,4,128,128]{4,3,2,1,0:T(8,128)(2,1)S(1)} %get-tuple-element.8.recv), custom_call_target="tpu_custom_call" | custom-call | tf_op jit(solution)/shard_map/pallas_call | solution.py:365
  202.6 30.5 %shard_map.48 = f32[24,768]{1,0:T(8,128)S(1)} custom-call(f32[4,2,2,2,24,768]{5,4,3,2,1,0:T(8,128)S(1)} %bitcast.24), custom_call_target="tpu_custom_call" | custom-call | tf_op jit(solution)/shard_map/pallas_call | solution.py:304
  233.1 0.6 copy.13
  (5 shorter events, 0.1 us)
Async XLA Ops:
  4.3 2.5 %copy-start = (bf16[40,4,128,128]{3,2,1,0:T(8,128)(2,1)S(1)}, bf16[40,4,128,128]{3,2,1,0:T(8,128)(2,1)}, u32[]{:S(2)}) copy-start(bf16[40,4,128,128]{3,2,1,0:T(8,128)(2,1)} %integrals.1) | copy-start | bytes 15728644
  6.8 0.9 copy-start.1
